TPU v7x, 512 devices: a whole 4x4x16 slice. The times are simulated.
512 devices in a mesh: seq: 64 (over y, z), head: 8 (over x, core).
Axes of the slice: x: 4, y: 4, z: 16, core: 2. Of those that a mesh axis runs over, the one named last changes fastest.
Arguments:
- queries: bfloat16 [128, 4096], P(None, 'head'), may hold values from -400 to 400
- keys: bfloat16 [16384, 1024], P('seq', 'head'), may hold values from -6 to 6
- values: bfloat16 [16384, 1024], P('seq', 'head'), may hold values from -6 to 6
- householder: bfloat16 [16384, 1024], P('seq', 'head'), may hold values from -6 to 6
- out_proj: bfloat16 [4096, 4096], P('head', 'seq'), may hold values from -0.09375 to 0.09375
Outputs:
- mixed: bfloat16 [128, 4096], P('head', 'seq')
All inputs are finite; a program needn't handle non-finite values.
Results may differ from a plain program's by a relative error of at most 0.02.
Values may be sent and summed in bfloat16 or wider, within the bound.
A program may use at most 64 MiB of HBM per device.

v0:
```python
import jax
import jax.numpy as jnp
from jax import lax
from jax.sharding import PartitionSpec as P

BLOCK = 64


def merged(array, axis, combine):
    everything = jax.tree.map(lambda part: lax.all_gather(part, axis), array)
    initial = jax.tree.map(lambda part: part[0], everything)

    def turn(k, so_far):
        return combine(so_far, jax.tree.map(lambda part: part[k], everything))

    return lax.fori_loop(1, lax.axis_size(axis), turn, initial)


def unit_rows(raw_vecs):
    return raw_vecs * lax.rsqrt(jnp.sum(raw_vecs * raw_vecs, axis=-1, keepdims=True) + 1e-06)


def span_forms(raw_vecs, keys_float):
    precise = lax.Precision.HIGHEST
    vectors = unit_rows(raw_vecs)
    block_len = vectors.shape[1]
    head_width = vectors.shape[2]
    row_ids = lax.broadcasted_iota(jnp.int32, (block_len, block_len), 0)
    col_ids = lax.broadcasted_iota(jnp.int32, (block_len, block_len), 1)
    gram = jnp.einsum("nad,nbd->nab", vectors, vectors, precision=precise)
    lower = jnp.where(row_ids > col_ids, gram, 0.0) + jnp.where(row_ids == col_ids, 0.5, 0.0)
    identity_block = jnp.broadcast_to(jnp.eye(block_len, dtype=jnp.float32), lower.shape)
    coeff = jax.scipy.linalg.solve_triangular(lower, identity_block, lower=True)
    identity_head = jnp.eye(head_width, dtype=jnp.float32)
    transition = identity_head - jnp.einsum(
        "nad,nab,nbe->nde", vectors, coeff, vectors, precision=precise
    )
    inner = jnp.einsum("nbd,njd->nbj", vectors, keys_float, precision=precise)
    inner = jnp.where(row_ids > col_ids, inner, 0.0)
    mixing = jnp.einsum("nab,nbj->naj", coeff, inner, precision=precise)
    carried = keys_float - jnp.einsum("naj,nad->njd", mixing, vectors, precision=precise)
    return (transition, carried)


def carry_back(transition, carried, identity_head):
    precise = lax.Precision.HIGHEST

    def advance(running, span_item):
        factor, block_keys = span_item
        emitted = jnp.dot(block_keys, running.T, precision=precise)
        return (jnp.dot(running, factor, precision=precise), emitted)

    return lax.scan(advance, identity_head, (transition, carried), reverse=True)


def compose_batch(earlier, later):
    return jnp.einsum("nab,nbc->nac", earlier, later, precision=lax.Precision.HIGHEST)


def combine_parts(first, second):
    peak_one, total_one, numer_one = first
    peak_two, total_two, numer_two = second
    peak = jnp.maximum(peak_one, peak_two)
    factor_one = jnp.exp(peak_one - peak)
    factor_two = jnp.exp(peak_two - peak)
    return (
        peak,
        total_one * factor_one + total_two * factor_two,
        numer_one * factor_one[..., None] + numer_two * factor_two[..., None],
    )


def on_device(queries, keys, values, householder, out_proj):
    precise = lax.Precision.HIGHEST
    ctx_rows, head_width = keys.shape
    blocks = ctx_rows // BLOCK
    raw_vecs = householder.astype(jnp.float32).reshape(blocks, BLOCK, head_width)
    keys_float = keys.astype(jnp.float32).reshape(blocks, BLOCK, head_width)
    transition, carried = span_forms(raw_vecs, keys_float)
    identity_head = jnp.eye(head_width, dtype=jnp.float32)
    shard_mat, local_keys = carry_back(transition, carried, identity_head)
    local_keys = local_keys.reshape(ctx_rows, head_width)
    all_trans = lax.all_gather(shard_mat[None], "seq", axis=0, tiled=True)
    my_index = lax.axis_index("seq")
    inclusive = lax.associative_scan(compose_batch, all_trans, reverse=True)
    padded_stack = jnp.concatenate([inclusive, identity_head[None]], axis=0)
    suffix_mat = lax.dynamic_index_in_dim(padded_stack, my_index + 1, 0, keepdims=False)
    query_count = queries.shape[0]
    group_size = queries.shape[1] // head_width
    query_float = queries.astype(jnp.float32).reshape(query_count, group_size, head_width)
    turned = jnp.einsum("ihe,ef->hif", query_float, suffix_mat, precision=precise)
    inv_root = 1.0 / jnp.sqrt(jnp.float32(head_width))

    def attend(query_rows):
        scores = jnp.einsum("if,jf->ij", query_rows, local_keys, precision=precise) * inv_root
        peak = jnp.max(scores, axis=1)
        expo = jnp.exp(scores - peak[:, None])
        totals = jnp.sum(expo, axis=1)
        numerators = jnp.dot(expo.astype(jnp.bfloat16), values, preferred_element_type=jnp.float32)
        return (peak, totals, numerators)

    peaks, totals, numerators = lax.map(attend, turned)
    best, merged_total, merged_numer = merged((peaks, totals, numerators), "seq", combine_parts)
    attention = (merged_numer / merged_total[..., None]).astype(jnp.bfloat16)
    flat_attention = jnp.transpose(attention, (1, 0, 2)).reshape(
        query_count, group_size * head_width
    )
    return lax.psum_scatter(
        jnp.dot(flat_attention, out_proj, preferred_element_type=jnp.float32).astype(jnp.bfloat16),
        "head",
        scatter_dimension=0,
        tiled=True,
    )


def solution(mesh):
    placed = (
        P(None, "head"),
        P("seq", "head"),
        P("seq", "head"),
        P("seq", "head"),
        P("head", "seq"),
    )
    return jax.shard_map(
        on_device, mesh=mesh, in_specs=placed, out_specs=P("head", "seq"), check_vma=False
    )
```

profile of v0, /device:TPU:8, one launch (start us, length us, event | category | flops | bytes accessed | tf_op | source)
XLA Modules:
  0.0 596.8 jit_solution(18420621423005850482)
XLA Ops:
  7.8 1.3 fusion.24
  9.1 19.7 %custom-call.4 = f32[4,1,64,64]{2,3,1,0:T(8,128)S(1)} custom-call(f32[4,1,64,64]{3,2,1,0:T(8,128)S(1)} %fusion.24), custom_call_target="InvertDiagBlocksLowerTriangular" | custom-call | tf_op jit(solution)/shard_map/jit(_solve_triangular)/vmap()/triangular_solve | solution.py:33
  30.3 1.3 fusion.50
  32.0 1.2 convolution_subtract_fusion.1
  33.9 2.1 while.49
  36.9 149.7 %all-gather.9.cloned.1.call-done = f32[8192,128]{1,0:T(8,128)} async-done(((f32[128,128]{1,0:T(8,128)}), f32[8192,128]{1,0:T(8,128)}) %all-gather.9.cloned.1.call-update) | async-done | bytes 4194320 | tf_op jit(solution)/shard_map/all_gather | solution.py:83
  186.6 3.1 slice.111
  189.8 1.7 slice.112
  191.5 3.7 fusion.18
  200.7 5.8 pad.43
  206.5 1.3 add.157
  210.0 10.2 %pad.46 = f32[32,128,128]{2,1,0:T(8,128)} pad(f32[16,128,128]{2,1,0:T(8,128)} %copy-done.3, f32[]{:T(128)} %constant.115.clone.1), padding=1_0_1x0_0_0x0_0_0 | pad | bytes 3145732 | tf_op jit(solution)/shard_map/pad | solution.py:85
  220.2 6.5 %pad.45 = f32[32,128,128]{2,1,0:T(8,128)} pad(f32[16,128,128]{2,1,0:T(8,128)S(1)} %pad_maximum_fusion.1, f32[]{:T(128)} %constant.115.clone.1), padding=0_1_1x0_0_0x0_0_0 | pad | bytes 3145732 | tf_op jit(solution)/shard_map/pad | solution.py:85
  226.7 2.5 add.158
  229.2 5.0 fusion.20
  234.2 12.1 %pad.48 = f32[64,128,128]{2,1,0:T(8,128)} pad(f32[32,128,128]{2,1,0:T(8,128)S(1)} %add.158, f32[]{:T(128)} %constant.115.clone.1), padding=1_0_1x0_0_0x0_0_0 | pad | bytes 6291460 | tf_op jit(solution)/shard_map/pad | solution.py:85
  247.1 1.7 pad_maximum_fusion
  248.8 12.1 %pad.47 = f32[64,128,128]{2,1,0:T(8,128)} pad(f32[32,128,128]{2,1,0:T(8,128)S(1)} %pad_maximum_fusion, f32[]{:T(128)} %constant.115.clone.1), padding=0_1_1x0_0_0x0_0_0 | pad | bytes 6291460 | tf_op jit(solution)/shard_map/pad | solution.py:85
  260.9 6.5 %add.159 = f32[64,128,128]{2,1,0:T(8,128)} add(f32[64,128,128]{2,1,0:T(8,128)} %pad.47, f32[64,128,128]{2,1,0:T(8,128)} %pad.48) | non-fusion elementwise | flops 1048576 | bytes 12582912 | tf_op jit(solution)/shard_map/add | solution.py:85
  267.4 4.6 rev.4
  273.3 6.0 %while.50 = (s32[]{:T(128)}, f32[4,128]{1,0:T(4,128)S(1)}, f32[4,128]{1,0:T(4,128)S(1)}, f32[4,128,128]{2,1,0:T(8,128)}, f32[4,128,128]{1,2,0:T(8,128)S(1)}, /*i...) while((s32[]{:T(128)}, f32[4,128]{1,0:T(4,128)S(1)}, ...), condition=%wide.region_6.7_spmd, body=%wide.region_3.6_spmd.sunk | while | flops 58916608 | bytes 725109 | solution.py:102
  279.3 97.9 %all-gather.4 = f32[64,4,128]{2,1,0:T(4,128)S(1)} all-gather(f32[1,4,128]{2,1,0:T(4,128)S(1)} %bitcast.152), channel_id=3, replica_groups=mesh['seq'=64,'head'=8] {'seq'}, dimensions={0}, use_global_device_ids=true | all-gather | bytes 133120 | tf_op jit(solution)/shard_map/all_gather | solution.py:10
  377.2 98.0 %all-gather.5 = f32[64,4,128]{2,1,0:T(4,128)S(1)} all-gather(f32[1,4,128]{2,1,0:T(4,128)S(1)} %bitcast.151), channel_id=4, replica_groups=mesh['seq'=64,'head'=8] {'seq'}, dimensions={0}, use_global_device_ids=true | all-gather | bytes 133120 | tf_op jit(solution)/shard_map/all_gather | solution.py:10
  476.2 79.3 %while.51 = (s32[]{:T(128)}, f32[4,128]{1,0:T(4,128)S(1)}, f32[4,128]{1,0:T(4,128)S(1)}, f32[4,128,128]{2,1,0:T(8,128)S(1)}, f32[64,4,128]{2,1,0:T(4,128)S(1)}, ...) while((s32[]{:T(128)}, f32[4,128]{1,0:T(4,128)S(1)}, ...), condition=%wide.region_8.9_spmd, body=%wide.region_7.8_spmd.sunk | while | flops 199685 | bytes 807055 | solution.py:16
  476.3 1.2 fusion.125
  477.5 1.2 fusion.125
  478.8 1.2 fusion.125
  480.0 1.2 fusion.125
  481.3 1.2 fusion.125
  482.6 1.2 fusion.125
  483.8 1.2 fusion.125
  556.6 33.7 %reduce-scatter.2.cloned.1.call-done = bf16[16,64]{1,0:T(8,128)(2,1)} async-done(((bf16[128,64]{1,0:T(8,128)(2,1)}), bf16[16,64]{1,0:T(8,128)(2,1)}) %reduce-scatter.2.cloned.1.call-update) | async-done | bytes 2064 | tf_op jit(solution)/shard_map/reduce_scatter | solution.py:108
  (225 shorter events, 93.5 us)
Async XLA Ops:
  6.5 265.5 %copy-start = (bf16[128,512]{1,0:T(8,128)(2,1)S(1)}, bf16[128,512]{1,0:T(8,128)(2,1)}, u32[]{:S(2)}) copy-start(bf16[128,512]{1,0:T(8,128)(2,1)} %param.11) | copy-start | bytes 393220
  6.5 26.7 %copy-start.4 = (bf16[256,128]{1,0:T(8,128)(2,1)S(1)}, bf16[256,128]{1,0:T(8,128)(2,1)}, u32[]{:S(2)}) copy-start(bf16[256,128]{1,0:T(8,128)(2,1)} %param.14) | copy-start | bytes 196612
  6.5 180.1 %all-gather.9.cloned.1.call-start = ((), (), s32[]{:S(2)}) async-start(), calls=%async_computation.2 | async-start | bytes 4259840 | tf_op jit(solution)/shard_map/all_gather | solution.py:83
  36.8 438.4 %all-gather.11.cloned.1.call-start = ((), (), s32[]{:S(2)}) async-start(), calls=%async_computation.3 | async-start | bytes 17039360 | tf_op jit(solution)/shard_map/all_gather | solution.py:10
  195.2 1.9 copy-start.1
  200.7 8.2 %copy-start.2 = (f32[32,128,128]{2,1,0:T(8,128)S(1)}, f32[32,128,128]{2,1,0:T(8,128)}, u32[]{:S(2)}) copy-start(f32[32,128,128]{2,1,0:T(8,128)} %copy-done.1) | copy-start | bytes 6291460
  207.8 1.1 copy-start.3
  210.0 10.2 %slice-start = ((f32[32,128,128]{2,1,0:T(8,128)}), f32[1,128,128]{2,1,0:T(8,128)S(1)}, s32[]{:S(2)}) async-start(f32[32,128,128]{2,1,0:T(8,128)} %copy-done.1), calls=%async_computation.4 | async-start | bytes 131072 | tf_op jit(solution)/shard_map/slice | solution.py:85
  272.1 1.2 copy-start.5
  279.3 310.9 %reduce-scatter.2.cloned.1.call-start = ((), (), s32[]{:S(2)}) async-start(), calls=%async_computation.1 | async-start | bytes 36864 | tf_op jit(solution)/shard_map/reduce_scatter | solution.py:108
  476.2 79.5 %copy-start.6 = (bf16[512,64]{0,1:T(8,128)(2,1)S(1)}, bf16[512,64]{0,1:T(8,128)(2,1)}, u32[]{:S(2)}) copy-start(bf16[512,64]{0,1:T(8,128)(2,1)} %param.15) | copy-start | bytes 196612
Sparse Core Ops, SparseCore 0:
  36.9 149.6 all-gather.8
  279.4 188.8 all-gather.10
  556.7 33.5 reduce-scatter.1
where the time goes:
time: 600 us; the launch traced here: 597 us
  blocking collectives  196 us (33%)
  waiting for transfers between devices  183 us (30%)
  other arithmetic  112 us (19%)
  local copies, waits for them, and re-layouts  60.8 us (10%)
  matrix products  28.9 us (5%)
  between operations  13.6 us (2%)
    all_gather x2, blocking collectives, merged(): everything = jax.tree.map(lambda part: lax.all_gather(part, axis), array)  196 us
    all_gather x1, waiting for transfers between devices, on_device(): all_trans = lax.all_gather(shard_mat[None], 'seq', axis=0, tiled=True)  150 us
    add x63, other arithmetic, combine_parts(): numer_one * factor_one[..., None] + numer_two * factor_two[..., None]  76 us
    pad x10, local copies, waits for them, and re-layouts, on_device(): inclusive = lax.associative_scan(compose_batch, all_trans, reverse=True)  47.1 us
    reduce_scatter x1, waiting for transfers between devices, on_device(): lax.psum_scatter(jnp.dot(flat_attention, out_proj, preferred_element_type...  33.7 us
    another operation x1, other arithmetic, span_forms(): coeff = jax.scipy.linalg.solve_triangular(lower, identity_block, lower=True)  19.7 us
    dot_general x11, matrix products, compose_batch(): jnp.einsum('nab,nbc->nac', earlier, later, precision=lax.Precision.HIGHEST)  13.6 us
  transfers between devices with their start and end apart: 3, of which 2 were waited for; matrix products, arithmetic and copies ran while one was open for 0% of the time, Pallas kernels for 0%

commit v1 on v0

--- a/solution.py
+++ b/solution.py
@@ -80,7 +80,11 @@
     identity_head = jnp.eye(head_width, dtype=jnp.float32)
     shard_mat, local_keys = carry_back(transition, carried, identity_head)
     local_keys = local_keys.reshape(ctx_rows, head_width)
-    all_trans = lax.all_gather(shard_mat[None], "seq", axis=0, tiled=True)
+    unit_supply_all = lambda inp, axis_id, which_dim: jnp.concatenate(
+        lax.all_to_all(jnp.stack([inp for _ in range(lax.axis_size(axis_id))]), axis_id, 0, 0),
+        axis=which_dim,
+    )
+    all_trans = unit_supply_all(shard_mat[None], "seq", 0)
     my_index = lax.axis_index("seq")
     inclusive = lax.associative_scan(compose_batch, all_trans, reverse=True)
     padded_stack = jnp.concatenate([inclusive, identity_head[None]], axis=0)

time: 600 us -> 657 us (1.095)
  waiting for transfers between devices: 183 us -> 218 us
  starting transfers between devices: 0.09 us -> 19 us
    all_to_all x0 -> x1, waiting for transfers between devices: none -> 185 us  [on_device(): lax.all_to_all(jnp.stack([inp for _ in range(lax.axis_size(axis_id))]), a...]
    all_gather x1 -> x0, waiting for transfers between devices: 150 us -> none  [on_device(): all_trans = lax.all_gather(shard_mat[None], 'seq', axis=0, tiled=True)]
    all_to_all x0 -> x1, starting transfers between devices: none -> 18.9 us  [on_device(): lax.all_to_all(jnp.stack([inp for _ in range(lax.axis_size(axis_id))]), a...]
where the time goes in v1:
time: 657 us; the launch traced here: 653 us
  waiting for transfers between devices  218 us (33%)
  blocking collectives  197 us (30%)
  other arithmetic  112 us (17%)
  local copies, waits for them, and re-layouts  62.2 us (9%)
  matrix products  28.9 us (4%)
  starting transfers between devices  19 us (3%)
  between operations  13.9 us (2%)
    all_gather x2, blocking collectives, merged(): everything = jax.tree.map(lambda part: lax.all_gather(part, axis), array)  197 us
    all_to_all x1, waiting for transfers between devices, on_device(): lax.all_to_all(jnp.stack([inp for _ in range(lax.axis_size(axis_id))]), a...  185 us
    add x63, other arithmetic, combine_parts(): numer_one * factor_one[..., None] + numer_two * factor_two[..., None]  76 us
    pad x10, local copies, waits for them, and re-layouts, on_device(): inclusive = lax.associative_scan(compose_batch, all_trans, reverse=True)  46.6 us
    reduce_scatter x1, waiting for transfers between devices, on_device(): lax.psum_scatter(jnp.dot(flat_attention, out_proj, preferred_element_type...  32.9 us
    another operation x1, other arithmetic, span_forms(): coeff = jax.scipy.linalg.solve_triangular(lower, identity_block, lower=True)  19.7 us
    all_to_all x1, starting transfers between devices, on_device(): lax.all_to_all(jnp.stack([inp for _ in range(lax.axis_size(axis_id))]), a...  18.9 us
    dot_general x11, matrix products, compose_batch(): jnp.einsum('nab,nbc->nac', earlier, later, precision=lax.Precision.HIGHEST)  13.6 us
  transfers between devices with their start and end apart: 3, of which 2 were waited for; matrix products, arithmetic and copies ran while one was open for 0% of the time, Pallas kernels for 0%

profile of v1, /device:TPU:8, one launch (start us, length us, event | category | flops | bytes accessed | tf_op | source)
XLA Modules:
  0.0 653.1 jit_solution(17366369527711899491)
XLA Ops:
  7.8 1.3 fusion.24
  9.1 19.7 %custom-call.4 = f32[4,1,64,64]{2,3,1,0:T(8,128)S(1)} custom-call(f32[4,1,64,64]{3,2,1,0:T(8,128)S(1)} %fusion.24), custom_call_target="InvertDiagBlocksLowerTriangular" | custom-call | tf_op jit(solution)/shard_map/jit(_solve_triangular)/vmap()/triangular_solve | solution.py:33
  30.3 1.3 fusion.50
  32.0 1.2 convolution_subtract_fusion.1
  33.9 2.1 while.49
  36.1 2.5 stack.3
  38.6 18.9 %all-to-all-start = ((f32[64,1,128,128]{3,2,1,0:T(8,128)}), f32[64,1,128,128]{3,2,1,0:T(8,128)}, u32[]{:S(2)}, u32[]{:S(2)}) async-start(f32[64,1,128,128]{3,2,1,0:T(8,128)} %stack.3), calls=%async_computation | async-start | bytes 8388608 | tf_op jit(solution)/shard_map/all_to_all | solution.py:84
  57.7 185.3 %all-to-all-done = f32[64,1,128,128]{3,2,1,0:T(8,128)} async-done(((f32[64,1,128,128]{3,2,1,0:T(8,128)}), f32[64,1,128,128]{3,2,1,0:T(8,128)}, u32[]{:S(2)}, u32[]{:S(2)}) %all-to-all-start) | async-done | bytes 4194336 | tf_op jit(solution)/shard_map/all_to_all | solution.py:84
  243.0 3.1 slice.115
  246.1 1.7 slice.116
  247.9 3.7 fusion.18
  257.1 5.7 pad.43
  262.8 1.3 add.157
  266.3 10.1 %pad.46 = f32[32,128,128]{2,1,0:T(8,128)} pad(f32[16,128,128]{2,1,0:T(8,128)} %copy-done.3, f32[]{:T(128)} %constant.115.clone.1), padding=1_0_1x0_0_0x0_0_0 | pad | bytes 3145732 | tf_op jit(solution)/shard_map/pad | solution.py:89
  276.6 6.3 pad.45
  282.9 2.5 add.158
  285.4 5.0 fusion.20
  290.3 12.0 %pad.48 = f32[64,128,128]{2,1,0:T(8,128)} pad(f32[32,128,128]{2,1,0:T(8,128)S(1)} %add.158, f32[]{:T(128)} %constant.115.clone.1), padding=1_0_1x0_0_0x0_0_0 | pad | bytes 6291460 | tf_op jit(solution)/shard_map/pad | solution.py:89
  303.1 1.7 pad_maximum_fusion
  304.8 11.9 %pad.47 = f32[64,128,128]{2,1,0:T(8,128)} pad(f32[32,128,128]{2,1,0:T(8,128)S(1)} %pad_maximum_fusion, f32[]{:T(128)} %constant.115.clone.1), padding=0_1_1x0_0_0x0_0_0 | pad | bytes 6291460 | tf_op jit(solution)/shard_map/pad | solution.py:89
  316.8 6.5 add.159
  323.3 4.6 rev.4
  329.1 6.0 while.50
  335.2 99.5 %all-gather.3 = f32[64,4,128]{2,1,0:T(4,128)S(1)} all-gather(f32[1,4,128]{2,1,0:T(4,128)S(1)} %bitcast.149), channel_id=2, replica_groups=mesh['seq'=64,'head'=8] {'seq'}, dimensions={0}, use_global_device_ids=true | all-gather | bytes 133120 | tf_op jit(solution)/shard_map/all_gather | solution.py:10
  434.8 97.4 %all-gather.4 = f32[64,4,128]{2,1,0:T(4,128)S(1)} all-gather(f32[1,4,128]{2,1,0:T(4,128)S(1)} %bitcast.148), channel_id=3, replica_groups=mesh['seq'=64,'head'=8] {'seq'}, dimensions={0}, use_global_device_ids=true | all-gather | bytes 133120 | tf_op jit(solution)/shard_map/all_gather | solution.py:10
  533.2 79.1 %while.51 = (s32[]{:T(128)}, f32[4,128]{1,0:T(4,128)S(1)}, f32[4,128]{1,0:T(4,128)S(1)}, f32[4,128,128]{2,1,0:T(8,128)S(1)}, f32[64,4,128]{2,1,0:T(4,128)S(1)}, ...) while((s32[]{:T(128)}, f32[4,128]{1,0:T(4,128)S(1)}, ...), condition=%wide.region_8.9_spmd, body=%wide.region_7.8_spmd.sunk | while | flops 199685 | bytes 807055 | solution.py:16
  533.3 1.2 fusion.125
  534.5 1.2 fusion.125
  535.8 1.2 fusion.125
  538.3 1.2 fusion.125
  539.5 1.2 fusion.125
  613.4 32.9 %reduce-scatter.2.cloned.1.call-done = bf16[16,64]{1,0:T(8,128)(2,1)} async-done(((bf16[128,64]{1,0:T(8,128)(2,1)}), bf16[16,64]{1,0:T(8,128)(2,1)}) %reduce-scatter.2.cloned.1.call-update) | async-done | bytes 2064 | tf_op jit(solution)/shard_map/reduce_scatter | solution.py:112
  (225 shorter events, 95.1 us)
Async XLA Ops:
  6.5 321.4 %copy-start = (bf16[128,512]{1,0:T(8,128)(2,1)S(1)}, bf16[128,512]{1,0:T(8,128)(2,1)}, u32[]{:S(2)}) copy-start(bf16[128,512]{1,0:T(8,128)(2,1)} %param.11) | copy-start | bytes 393220
  6.5 26.7 %copy-start.4 = (bf16[256,128]{1,0:T(8,128)(2,1)S(1)}, bf16[256,128]{1,0:T(8,128)(2,1)}, u32[]{:S(2)}) copy-start(bf16[256,128]{1,0:T(8,128)(2,1)} %param.14) | copy-start | bytes 196612
  38.6 204.4 %all-to-all-start = ((f32[64,1,128,128]{3,2,1,0:T(8,128)}), f32[64,1,128,128]{3,2,1,0:T(8,128)}, u32[]{:S(2)}, u32[]{:S(2)}) async-start(f32[64,1,128,128]{3,2,1,0:T(8,128)} %stack.3), calls=%async_computation | async-start | bytes 8388608 | tf_op jit(solution)/shard_map/all_to_all | solution.py:84
  57.5 474.7 %all-gather.7.cloned.1.call-start = ((), (), s32[]{:S(2)}) async-start(), calls=%async_computation.3 | async-start | bytes 17039360 | tf_op jit(solution)/shard_map/all_gather | solution.py:10
  251.6 1.9 copy-start.1
  257.1 8.1 %copy-start.2 = (f32[32,128,128]{2,1,0:T(8,128)S(1)}, f32[32,128,128]{2,1,0:T(8,128)}, u32[]{:S(2)}) copy-start(f32[32,128,128]{2,1,0:T(8,128)} %copy-done.1) | copy-start | bytes 6291460
  264.1 1.1 copy-start.3
  266.3 10.2 %slice-start = ((f32[32,128,128]{2,1,0:T(8,128)}), f32[1,128,128]{2,1,0:T(8,128)S(1)}, s32[]{:S(2)}) async-start(f32[32,128,128]{2,1,0:T(8,128)} %copy-done.1), calls=%async_computation.4 | async-start | bytes 131072 | tf_op jit(solution)/shard_map/slice | solution.py:89
  327.9 1.2 copy-start.5
  335.2 311.1 %reduce-scatter.2.cloned.1.call-start = ((), (), s32[]{:S(2)}) async-start(), calls=%async_computation.2 | async-start | bytes 36864 | tf_op jit(solution)/shard_map/reduce_scatter | solution.py:112
  533.2 79.3 %copy-start.6 = (bf16[512,64]{0,1:T(8,128)(2,1)S(1)}, bf16[512,64]{0,1:T(8,128)(2,1)}, u32[]{:S(2)}) copy-start(bf16[512,64]{0,1:T(8,128)(2,1)} %param.15) | copy-start | bytes 196612
Sparse Core Ops, SparseCore 0:
  335.3 188.9 all-gather.6
  613.5 32.6 reduce-scatter.1
